TPU v7x, 256 devices: a whole 4x4x8 slice. The times are simulated.
256 devices in a mesh: pair: 2 (over y_hi), ctx: 8 (over x, core), batch: 16 (over z, y_lo).
Axes of the slice: x: 4, y: 4 (y_hi: 2, y_lo: 2; y = y_hi * 2 + y_lo), z: 8, core: 2. Of those that a mesh axis runs over, the one named last changes fastest.
Arguments:
- prompt_keys: bfloat16 [49152, 512], P(('batch', 'pair', 'ctx')), parts along dimension 0, may hold values from -5 to 5
- prompt_values: bfloat16 [49152, 512], P(('batch', 'pair', 'ctx')), parts along dimension 0, may hold values from -6 to 6
- resp_queries: bfloat16 [2, 16384, 2048], P('pair', ('batch', 'ctx')), parts along dimension 1, may hold values from -100 to 100
- resp_keys: bfloat16 [2, 16384, 512], P('pair', ('batch', 'ctx')), parts along dimension 1, may hold values from -6 to 6
- resp_values: bfloat16 [2, 16384, 512], P('pair', ('batch', 'ctx')), parts along dimension 1, may hold values from -6 to 6
- out_grad: bfloat16 [2, 16384, 2048], P('pair', ('batch', 'ctx')), parts along dimension 1, may hold values from -6 to 6
- lengths: int32 [32], P(('batch', 'pair')), parts along dimension 0, may hold values from 256 to 1024, as said below
Outputs:
- attn_out: bfloat16 [2, 16384, 2048], P('pair', ('batch', 'ctx')), parts along dimension 1
- query_grad: bfloat16 [2, 16384, 2048], P('pair', ('batch', 'ctx')), parts along dimension 1
- resp_key_grad: bfloat16 [2, 16384, 512], P('pair', ('batch', 'ctx')), parts along dimension 1
- resp_value_grad: bfloat16 [2, 16384, 512], P('pair', ('batch', 'ctx')), parts along dimension 1
- prompt_key_grad: bfloat16 [49152, 512], P(('batch', 'pair', 'ctx')), parts along dimension 0
- prompt_value_grad: bfloat16 [49152, 512], P(('batch', 'pair', 'ctx')), parts along dimension 0
There are 16 independent parts, one for each index of `batch`. A program takes and returns all parts, laid end to end along the dimension named above; each array names one. Nothing has to cross between parts.
Inputs may be any that keep to these rules, and one draw needn't show every extreme that they name: One of the two lengths is exactly 1024.
All inputs are finite; a program needn't handle non-finite values.
Results may differ from a plain program's by a relative error of at most 0.028.
Values may be sent and summed in bfloat16 or wider, within the bound.
No kernel may reach another device: no remote copies, remote signals or barrier semaphores. Data moves between devices by JAX's collectives and lax.ppermute only.
A program may use at most 128 MiB of HBM per device.

v0:
```python
import math

import jax
import jax.numpy as jnp
from jax import lax
from jax.experimental import pallas as pl
from jax.experimental.pallas import tpu as pltpu
from jax.sharding import PartitionSpec as P

F32 = jnp.float32
BF = jnp.bfloat16
SCALE = 1.0 / math.sqrt(128.0)
SCALE_LOG2 = math.log2(math.e) / math.sqrt(128.0)
CHIPS = 4
PROMPT_ROWS = 192
RESP_ROWS = 128
KEYS = 4096
PROMPT_KEYS = 3072
KEY_BLOCK = 1536
VMEM = pl.BlockSpec(memory_space=pltpu.VMEM)
SMEM = pl.BlockSpec(memory_space=pltpu.SMEM)


def dot(a, b):
    return jnp.dot(a, b, preferred_element_type=F32)


def shape(dims, dtype=BF):
    return jax.ShapeDtypeStruct(dims, dtype)


def lanes(index, width):
    return pl.ds(pl.multiple_of(index * width, width), width)


def pack_keys(place, pk, pv, rk, rv, *outs):
    x = place[2]
    for d in range(CHIPS):
        head = lanes(lax.rem(x + d, CHIPS), 128)
        outs[d][0:192, :] = pk[:, head]
        outs[d][192:384, :] = pv[:, head]
        outs[d][384:512, :] = rk[:, head]
        outs[d][512:640, :] = rv[:, head]


def pack_rows(place, q, g, *outs):
    x = place[2]
    for d in range(CHIPS):
        heads = lanes(lax.rem(x + d, CHIPS), 512)
        outs[d][0:128, :] = q[:, heads]
        outs[d][128:256, :] = g[:, heads]


def unpack_rows(place, *refs):
    x = place[2]
    oq, o, dq = refs[0:4], refs[4], refs[5]
    for d in range(CHIPS):
        heads = lanes(lax.rem(x + d, CHIPS), 512)
        o[:, heads] = oq[d][0:128, :]
        dq[:, heads] = oq[d][128:256, :]


def unpack_keys(place, *refs):
    x = place[2]
    pk, pv, rk, rv = refs[2 * CHIPS :]
    for d in range(CHIPS):
        head = lanes(lax.rem(x + d, CHIPS), 128)
        pk[:, head] = refs[d][0:PROMPT_ROWS, :]
        pv[:, head] = refs[d][PROMPT_ROWS:, :]
        rk[:, head] = refs[CHIPS + d][0:RESP_ROWS, :]
        rv[:, head] = refs[CHIPS + d][RESP_ROWS:, :]


def sum_prompt(own, other, far, *outs):
    for d in range(CHIPS):
        at = slice(384 * d, 384 * (d + 1))
        outs[d][...] = (own[at, :] + other[at, :].astype(F32) + far[at, :].astype(F32)).astype(BF)


def sum_resp(own, other, *outs):
    for d in range(CHIPS):
        at = slice(256 * d, 256 * (d + 1))
        far = slice(1536 + 256 * d, 1792 + 256 * d)
        outs[d][...] = (own[at, :] + other[far, :].astype(F32)).astype(BF)


def attention(place, *refs):
    qg_in = refs[0:4]
    own_in, other_in = refs[4:6]
    prompt_in = (own_in, other_in, refs[6], refs[7])
    oq_out = refs[8:12]
    own_out, resp_out, other_out = refs[12:15]
    dprompt_out = (own_out, other_out, refs[15], refs[16])
    (qs, gs, os_, qn, qT, gT, gn, kk, kT, vv, vT, sp, ee, ds_s, dq, dkp, dvp, dkr, dvr) = refs[17:]
    c, length, x = place[0], place[1], place[2]

    chip_of = [lax.rem(x + CHIPS - d, CHIPS) for d in range(CHIPS)]
    for d in range(CHIPS):
        qs[pl.ds(chip_of[d], 1)] = qg_in[d][0:128, :][None]
        gs[pl.ds(chip_of[d], 1)] = qg_in[d][128:256, :][None]
    for s in range(4):
        for d in range(CHIPS):
            at = slice(768 * s + PROMPT_ROWS * d, 768 * s + PROMPT_ROWS * (d + 1))
            off = 2 * PROMPT_ROWS * d
            kk[at, 0:128] = prompt_in[s][off : off + PROMPT_ROWS, :]
            vv[at, 0:128] = prompt_in[s][off + PROMPT_ROWS : off + 2 * PROMPT_ROWS, :]
    resp_at = []
    for s in range(2):
        for d in range(CHIPS):
            parity = c if s == 0 else 1 - c
            at = PROMPT_KEYS + (2 * chip_of[d] + parity) * RESP_ROWS
            at = pl.ds(pl.multiple_of(at, RESP_ROWS), RESP_ROWS)
            off = 1536 + 2 * RESP_ROWS * d
            kk[at, 0:128] = prompt_in[s][off : off + RESP_ROWS, :]
            vv[at, 0:128] = prompt_in[s][off + RESP_ROWS : off + 2 * RESP_ROWS, :]
    kk[:, 128:256] = kk[:, 0:128]
    kT[...] = kk[:, 0:128].T
    vT[0:128, :] = vv[:, 0:128].T
    vT[128:144, :] = jnp.ones((16, KEYS), BF)
    lane = lax.broadcasted_iota(jnp.int32, (KEYS, 128), 1)
    vv[:, 128:256] = jnp.where(lane < 2, 1.0, 0.0).astype(BF)
    for j in range(4):
        for h in range(4):
            q = qs[j, :, h * 128 : (h + 1) * 128]
            r0 = j * 512 + h * 128
            qn[r0 : r0 + 128, :] = q
            qc = q.T.astype(F32) * SCALE_LOG2
            hi = qc.astype(BF)
            qT[0:128, r0 : r0 + 128] = hi
            qT[128:256, r0 : r0 + 128] = (qc - hi.astype(F32)).astype(BF)

    def chunks(j):
        return [(512 * t, 512 * (t + 1)) for t in range(PROMPT_KEYS // 512)] + [
            (PROMPT_KEYS + 256 * t, PROMPT_KEYS + 256 * (t + 1)) for t in range(j + 1)
        ]

    tops, sums = [None] * 4, [None] * 4
    for j in range(5):
        now = chunks(j) if j < 4 else []
        before = chunks(j - 1) if j > 0 else []
        cols = slice(j * 512, (j + 1) * 512)
        cols_before = slice((j - 1) * 512, j * 512)
        for n in range(max(len(now), len(before))):
            if n < len(now):
                lo, hi = now[n]
                s = dot(kk[lo:hi, :], qT[:, cols])
                if n == len(now) - 1:
                    row = c * 128 + lax.rem(lax.broadcasted_iota(jnp.int32, (256, 512), 1), 128)
                    key = lax.broadcasted_iota(jnp.int32, (256, 512), 0)
                    s = jnp.where(key <= row, s, -jnp.inf)
                sp[j % 2, lo:hi, :] = s
                top = jnp.max(s, axis=0, keepdims=True)
                tops[j] = top if n == 0 else jnp.maximum(tops[j], top)
            if n < len(before):
                lo, hi = before[n]
                e = jnp.exp2(sp[(j - 1) % 2, lo:hi, :] - tops[j - 1]).astype(BF)
                ee[lo:hi, cols_before] = e
                part = dot(vT[:, lo:hi], e)
                sums[j - 1] = part if n == 0 else sums[j - 1] + part
    for j in range(4):
        a = sums[j]
        inv = 1.0 / a[128:129, :]
        lane = lax.broadcasted_iota(jnp.int32, (1, 512), 1)
        live = (2 * j + c) * 128 + lax.rem(lane, 128) < length
        oT = jnp.where(live, a[0:128, :] * inv, 0.0).astype(BF)
        for h in range(4):
            hs = slice(h * 128, (h + 1) * 128)
            r0 = j * 512 + h * 128
            o = oT[:, hs]
            os_[j, :, hs] = o.T
            gt = jnp.where(live[:, hs], gs[j, :, hs].T.astype(F32) * inv[:, hs], 0.0).astype(BF)
            row_dot = jnp.sum(gt.astype(F32) * o.astype(F32), axis=0, keepdims=True)
            gT[0:128, r0 : r0 + 128] = gt
            gn[r0 : r0 + 128, :] = gt.T
            high = row_dot.astype(BF).astype(F32)
            sub = lax.broadcasted_iota(jnp.int32, (128, 128), 0)
            gT[128:256, r0 : r0 + 128] = jnp.where(
                sub == 0, -high, jnp.where(sub == 1, high - row_dot, 0.0)
            ).astype(BF)

    def prompt_block(t, _):
        keys = pl.ds(pl.multiple_of(t * KEY_BLOCK, KEY_BLOCK), KEY_BLOCK)
        dp = dot(vv[keys, :], gT[...])
        ds_s[...] = (dp * ee[keys, :].astype(F32)).astype(BF)
        dvp[keys, :] = dot(ee[keys, :], gn[...])
        dkp[keys, :] = dot(ds_s[...], qn[...]) * SCALE
        part = dot(kT[:, keys], ds_s[...])

        @pl.when(t == 0)
        def _():
            dq[...] = part

        @pl.when(t > 0)
        def _():
            dq[...] += part

        return 0

    lax.fori_loop(0, PROMPT_KEYS // KEY_BLOCK, prompt_block, 0)
    for t in range(4):
        keys = slice(PROMPT_KEYS + 256 * t, PROMPT_KEYS + 256 * (t + 1))
        at = slice(256 * t, 256 * (t + 1))
        cols = slice(512 * t, 2048)
        e = ee[keys, cols]
        ds = (dot(vv[keys, :], gT[:, cols]) * e.astype(F32)).astype(BF)
        dvr[at, :] = dot(e, gn[cols, :])
        dkr[at, :] = dot(ds, qn[cols, :]) * SCALE
        dq[:, cols] += dot(kT[:, keys], ds)

    for s in range(4):
        for d in range(CHIPS):
            at = slice(768 * s + PROMPT_ROWS * d, 768 * s + PROMPT_ROWS * (d + 1))
            off = 2 * PROMPT_ROWS * d
            out = dprompt_out[s]
            out[off : off + PROMPT_ROWS, :] = dkp[at, :].astype(out.dtype)
            out[off + PROMPT_ROWS : off + 2 * PROMPT_ROWS, :] = dvp[at, :].astype(out.dtype)
    for s in range(2):
        for d in range(CHIPS):
            parity = c if s == 0 else 1 - c
            at = (2 * chip_of[d] + parity) * RESP_ROWS
            at = pl.ds(pl.multiple_of(at, RESP_ROWS), RESP_ROWS)
            off = 2 * RESP_ROWS * d + (1536 if s else 0)
            out = other_out if s else resp_out
            out[off : off + RESP_ROWS, :] = dkr[at, :].astype(out.dtype)
            out[off + RESP_ROWS : off + 2 * RESP_ROWS, :] = dvr[at, :].astype(out.dtype)
    for j in range(4):
        for h in range(4):
            r0 = j * 512 + h * 128
            qs[j, :, h * 128 : (h + 1) * 128] = (dq[:, r0 : r0 + 128] * SCALE).astype(BF).T
    for d in range(CHIPS):
        oq_out[d][0:128, :] = os_[pl.ds(chip_of[d], 1)][0]
        oq_out[d][128:256, :] = qs[pl.ds(chip_of[d], 1)][0]


def to_chip(a, d):
    return lax.ppermute(
        a, "ctx", [(2 * x + c, 2 * ((x + d) % CHIPS) + c) for x in range(CHIPS) for c in range(2)]
    )


def to_core(a):
    return lax.ppermute(a, "ctx", [(i, i ^ 1) for i in range(2 * CHIPS)])


def to_pair(a):
    return lax.ppermute(a, "pair", [(0, 1), (1, 0)])


def spread(parts, sign):
    return [parts[0]] + [to_chip(parts[d], sign * d) for d in range(1, CHIPS)]


def small(body, name, out_shape, n_in, scalars=True, limit=24):
    return pl.pallas_call(
        body,
        out_shape=out_shape,
        in_specs=([SMEM] if scalars else []) + [VMEM] * n_in,
        out_specs=[VMEM] * len(out_shape),
        compiler_params=pltpu.CompilerParams(vmem_limit_bytes=limit << 20),
        name=name,
    )


def per_device(prompt_keys, prompt_values, resp_queries, resp_keys, resp_values, out_grad, lengths):
    ctx = lax.axis_index("ctx")
    place = jnp.stack([ctx % 2, lengths[0], ctx // 2]).astype(jnp.int32)
    block = shape((640, 128))
    rows = shape((256, 512))
    far_block = (1536, 128)
    own_block = (2560, 128)

    packed = small(pack_keys, "pack_keys", [block] * 4, 4)(
        place, prompt_keys, prompt_values, resp_keys[0], resp_values[0]
    )
    kv = spread(packed, 1)
    packed = small(pack_rows, "pack_rows", [rows] * 4, 2)(place, resp_queries[0], out_grad[0])
    prompt = jnp.concatenate([k[:384] for k in kv], axis=0)
    own = jnp.concatenate([k[:384] for k in kv] + [k[384:] for k in kv], axis=0)
    far = to_pair(prompt)
    other = to_core(own)
    sent = lax.optimization_barrier(tuple(packed) + (prompt,))
    qg = spread(sent[:4], 1)
    held = lax.optimization_barrier((far, *qg))
    far, qg = held[0], held[1:]
    far_other = to_core(far)

    all_rows = 4 * 512
    outs = pl.pallas_call(
        attention,
        out_shape=[rows] * 4
        + [shape(far_block, F32), shape((1024, 128), F32), shape(own_block)]
        + [shape(far_block, F32), shape(far_block)],
        in_specs=[SMEM] + [VMEM] * 8,
        out_specs=[VMEM] * 9,
        scratch_shapes=[
            pltpu.VMEM((4, 128, 512), BF),
            pltpu.VMEM((4, 128, 512), BF),
            pltpu.VMEM((4, 128, 512), BF),
            pltpu.VMEM((all_rows, 128), BF),
            pltpu.VMEM((256, all_rows), BF),
            pltpu.VMEM((256, all_rows), BF),
            pltpu.VMEM((all_rows, 128), BF),
            pltpu.VMEM((KEYS, 256), BF),
            pltpu.VMEM((128, KEYS), BF),
            pltpu.VMEM((KEYS, 256), BF),
            pltpu.VMEM((144, KEYS), BF),
            pltpu.VMEM((2, KEYS, 512), F32),
            pltpu.VMEM((KEYS, all_rows), BF),
            pltpu.VMEM((KEY_BLOCK, all_rows), BF),
            pltpu.VMEM((128, all_rows), F32),
            pltpu.VMEM((PROMPT_KEYS, 128), F32),
            pltpu.VMEM((PROMPT_KEYS, 128), F32),
            pltpu.VMEM((1024, 128), F32),
            pltpu.VMEM((1024, 128), F32),
        ],
        compiler_params=pltpu.CompilerParams(vmem_limit_bytes=60 << 20),
        cost_estimate=pl.CostEstimate(
            flops=10 * 2048 * 3712 * 128, bytes_accessed=10 << 20, transcendentals=2048 * 3712
        ),
        name="attention",
    )(place, *qg, own, other, far, far_other)
    oq = outs[0:4]
    d_own, d_resp, d_other, d_far, d_far_other = outs[4:9]

    got_far = to_core(d_far_other)
    got_other = to_core(d_other)
    oq = spread(oq, -1)
    there = (d_far + got_far.astype(F32)).astype(BF)
    here = to_pair(there)
    dr = small(sum_resp, "sum_resp", [shape((256, 128))] * 4, 2, False)(d_resp, got_other)
    dr = spread(dr, -1)
    dp = small(sum_prompt, "sum_prompt", [shape((384, 128))] * 4, 3, False)(d_own, got_other, here)
    dp = spread(dp, -1)
    attn_out, query_grad = small(unpack_rows, "unpack_rows", [shape((128, 2048))] * 2, 4)(
        place, *oq
    )
    pk, pv, rk, rv = small(
        unpack_keys, "unpack_keys", [shape((192, 512))] * 2 + [shape((128, 512))] * 2, 8
    )(place, *dp, *dr)
    return attn_out[None], query_grad[None], rk[None], rv[None], pk, pv


def solution(mesh):
    placed = (
        P(("batch", "pair", "ctx"), None),
        P(("batch", "pair", "ctx"), None),
        P("pair", ("batch", "ctx"), None),
        P("pair", ("batch", "ctx"), None),
        P("pair", ("batch", "ctx"), None),
        P("pair", ("batch", "ctx"), None),
        P(("batch", "pair")),
    )
    return jax.shard_map(
        per_device,
        mesh=mesh,
        in_specs=placed,
        out_specs=(
            P("pair", ("batch", "ctx"), None),
            P("pair", ("batch", "ctx"), None),
            P("pair", ("batch", "ctx"), None),
            P("pair", ("batch", "ctx"), None),
            P(("batch", "pair", "ctx"), None),
            P(("batch", "pair", "ctx"), None),
        ),
        check_vma=False,
    )
```

profile of v0, /device:TPU:112, one launch (start us, length us, event | category | flops | bytes accessed | tf_op | source)
XLA Modules:
  0.0 101.4 jit_solution(15880320266945084580)
XLA Ops:
  1.4 0.1 pad_add_fusion.place
  1.4 0.9 copy-done.5
  2.4 0.9 copy-done.6
  3.3 0.9 copy-done.7
  4.2 0.9 copy-done.8
  5.1 0.7 pack_keys.1
  5.8 1.6 %collective-permute-start = (bf16[640,128]{1,0:T(8,128)(2,1)S(1)}, bf16[640,128]{1,0:T(8,128)(2,1)S(1)}, u32[]{:S(2)}, u32[]{:S(2)}) collective-permute-start(bf16[640,128]{1,0:T(8,128)(2,1)S(1)} %get-tuple-element.47), channel_id=1, source_target_pairs={{0,32},{16,48},{32,64},{48,80},{64,96},{80,112},{96,0},{112,16},{1... | collective-permute-start | bytes 491528 | tf_op jit(solution)/shard_map/ppermute | solution.py:236
  7.3 2.7 %collective-permute-start.1 = (bf16[640,128]{1,0:T(8,128)(2,1)S(1)}, bf16[640,128]{1,0:T(8,128)(2,1)S(1)}, u32[]{:S(2)}, u32[]{:S(2)}) collective-permute-start(bf16[640,128]{1,0:T(8,128)(2,1)S(1)} %get-tuple-element.48), channel_id=1, source_target_pairs={{0,64},{16,80},{32,96},{48,112},{64,0},{80,16},{96,32},{112,48},{1... | collective-permute-start | bytes 491528 | tf_op jit(solution)/shard_map/ppermute | solution.py:236
  10.1 1.4 %collective-permute-start.2 = (bf16[640,128]{1,0:T(8,128)(2,1)S(1)}, bf16[640,128]{1,0:T(8,128)(2,1)S(1)}, u32[]{:S(2)}, u32[]{:S(2)}) collective-permute-start(bf16[640,128]{1,0:T(8,128)(2,1)S(1)} %get-tuple-element.49), channel_id=1, source_target_pairs={{0,96},{16,112},{32,0},{48,16},{64,32},{80,48},{96,64},{112,80},{1... | collective-permute-start | bytes 491528 | tf_op jit(solution)/shard_map/ppermute | solution.py:236
  11.5 1.0 %copy-done.3 = bf16[1,128,2048]{2,1,0:T(8,128)(2,1)S(1)} copy-done((bf16[1,128,2048]{2,1,0:T(8,128)(2,1)S(1)}, bf16[1,128,2048]{2,1,0:T(8,128)(2,1)}, u32[]{:S(2)}) %copy-start.3) | copy-done | bytes 524312
  12.6 0.6 pack_rows.1
  13.3 0.6 copy-done.11
  13.9 3.6 %collective-permute-done.1 = bf16[640,128]{1,0:T(8,128)(2,1)S(1)} collective-permute-done((bf16[640,128]{1,0:T(8,128)(2,1)S(1)}, bf16[640,128]{1,0:T(8,128)(2,1)S(1)}, u32[]{:S(2)}, u32[]{:S(2)}) %collective-permute-start.1) | collective-permute-done | bytes 163872 | tf_op jit(solution)/shard_map/ppermute | solution.py:236
  17.6 0.4 collective-permute-start.3
  18.0 1.3 %collective-permute-start.4 = (bf16[256,512]{1,0:T(8,128)(2,1)S(1)}, bf16[256,512]{1,0:T(8,128)(2,1)S(1)}, u32[]{:S(2)}, u32[]{:S(2)}) collective-permute-start(bf16[256,512]{1,0:T(8,128)(2,1)S(1)} %get-tuple-element.55), channel_id=1, source_target_pairs={{0,32},{16,48},{32,64},{48,80},{64,96},{80,112},{96,0},{112,16},{1... | collective-permute-start | bytes 786440 | tf_op jit(solution)/shard_map/ppermute | solution.py:236
  19.3 2.4 %collective-permute-start.5 = (bf16[256,512]{1,0:T(8,128)(2,1)S(1)}, bf16[256,512]{1,0:T(8,128)(2,1)S(1)}, u32[]{:S(2)}, u32[]{:S(2)}) collective-permute-start(bf16[256,512]{1,0:T(8,128)(2,1)S(1)} %get-tuple-element.56), channel_id=1, source_target_pairs={{0,64},{16,80},{32,96},{48,112},{64,0},{80,16},{96,32},{112,48},{1... | collective-permute-start | bytes 786440 | tf_op jit(solution)/shard_map/ppermute | solution.py:236
  21.7 1.6 %collective-permute-start.6 = (bf16[256,512]{1,0:T(8,128)(2,1)S(1)}, bf16[256,512]{1,0:T(8,128)(2,1)S(1)}, u32[]{:S(2)}, u32[]{:S(2)}) collective-permute-start(bf16[256,512]{1,0:T(8,128)(2,1)S(1)} %get-tuple-element.57), channel_id=1, source_target_pairs={{0,96},{16,112},{32,0},{48,16},{64,32},{80,48},{96,64},{112,80},{1... | collective-permute-start | bytes 786440 | tf_op jit(solution)/shard_map/ppermute | solution.py:236
  23.4 0.1 collective-permute-start.7
  23.5 3.9 %collective-permute-done.4.refs_1_ = bf16[256,512]{1,0:T(8,128)(2,1)S(1)} collective-permute-done((bf16[256,512]{1,0:T(8,128)(2,1)S(1)}, bf16[256,512]{1,0:T(8,128)(2,1)S(1)}, u32[]{:S(2)}, u32[]{:S(2)}) %collective-permute-start.4) | collective-permute-done | bytes 262176 | tf_op jit(solution)/shard_map/ppermute | solution.py:236
  27.4 5.2 %collective-permute-done.5.refs_2_ = bf16[256,512]{1,0:T(8,128)(2,1)S(1)} collective-permute-done((bf16[256,512]{1,0:T(8,128)(2,1)S(1)}, bf16[256,512]{1,0:T(8,128)(2,1)S(1)}, u32[]{:S(2)}, u32[]{:S(2)}) %collective-permute-start.5) | collective-permute-done | bytes 262176 | tf_op jit(solution)/shard_map/ppermute | solution.py:236
  32.6 0.0 copy-start.14
  32.6 0.3 collective-permute-start.8
  32.9 0.0 collective-permute-done.7.refs_5_
  32.9 1.7 %collective-permute-done.8.refs_7_ = bf16[1536,128]{1,0:T(8,128)(2,1)S(1)} collective-permute-done((bf16[1536,128]{1,0:T(8,128)(2,1)S(1)}, bf16[1536,128]{1,0:T(8,128)(2,1)S(1)}, u32[]{:S(2)}, u32[]{:S(2)}) %collective-permute-start.8) | collective-permute-done | bytes 393248 | tf_op jit(solution)/shard_map/ppermute | solution.py:242
  34.7 0.8 copy-done.15
  35.4 32.0 %attention.1 = (bf16[256,512]{1,0:T(8,128)(2,1)}, bf16[256,512]{1,0:T(8,128)(2,1)}, bf16[256,512]{1,0:T(8,128)(2,1)}, bf16[256,512]{1,0:T(8,128)(2,1)}, f32[1536...) custom-call(s32[3]{0:T(128)} %copy-done.9, ...), custom_call_target="tpu_custom_call" | custom-call | flops 9730785280 | bytes 10485760 | tf_op jit(solution)/shard_map/attention/pallas_call | solution.py:288
  67.4 0.1 collective-permute-start.13
  67.5 0.4 collective-permute-start.12
  67.9 1.4 %collective-permute-done.13 = bf16[1536,128]{1,0:T(8,128)(2,1)S(1)} collective-permute-done((bf16[1536,128]{1,0:T(8,128)(2,1)}, bf16[1536,128]{1,0:T(8,128)(2,1)S(1)}, u32[]{:S(2)}, u32[]{:S(2)}) %collective-permute-start.13) | collective-permute-done | bytes 393248 | tf_op jit(solution)/shard_map/ppermute | solution.py:242
  69.4 1.3 %add_convert_fusion = bf16[1536,128]{1,0:T(8,128)(2,1)S(1)} fusion(f32[1536,128]{1,0:T(8,128)} %get-tuple-element.71, bf16[1536,128]{1,0:T(8,128)(2,1)S(1)} %collective-permute-done.13), kind=kLoop, calls=%fused_computation | loop fusion | flops 589824 | bytes 1572864 | tf_op jit(solution)/shard_map/convert_element_type | solution.py:328
  70.7 3.2 %collective-permute-start.14 = (bf16[1536,128]{1,0:T(8,128)(2,1)S(1)}, bf16[1536,128]{1,0:T(8,128)(2,1)S(1)}, u32[]{:S(2)}, u32[]{:S(2)}) collective-permute-start(bf16[1536,128]{1,0:T(8,128)(2,1)S(1)} %add_convert_fusion), channel_id=1, source_target_pairs={{0,128},{128,0},{1,129},{129,1},{2,130},{130,2},{3,131},{131,3},{4... | collective-permute-start | bytes 1179656 | tf_op jit(solution)/shard_map/ppermute | solution.py:246
  73.9 2.4 %collective-permute-start.9 = (bf16[256,512]{1,0:T(8,128)(2,1)S(1)}, bf16[256,512]{1,0:T(8,128)(2,1)S(1)}, u32[]{:S(2)}, u32[]{:S(2)}) collective-permute-start(bf16[256,512]{1,0:T(8,128)(2,1)S(1)} %copy-done.18), channel_id=1, source_target_pairs={{0,96},{16,112},{32,0},{48,16},{64,32},{80,48},{96,64},{112,80},{1... | collective-permute-start | bytes 786440 | tf_op jit(solution)/shard_map/ppermute | solution.py:236
  76.4 1.2 %collective-permute-start.10 = (bf16[256,512]{1,0:T(8,128)(2,1)S(1)}, bf16[256,512]{1,0:T(8,128)(2,1)S(1)}, u32[]{:S(2)}, u32[]{:S(2)}) collective-permute-start(bf16[256,512]{1,0:T(8,128)(2,1)S(1)} %copy-done.17), channel_id=1, source_target_pairs={{0,64},{16,80},{32,96},{48,112},{64,0},{80,16},{96,32},{112,48},{1... | collective-permute-start | bytes 786440 | tf_op jit(solution)/shard_map/ppermute | solution.py:236
  77.6 0.0 collective-permute-start.11
  77.6 3.6 %collective-permute-start.18 = (bf16[256,128]{1,0:T(8,128)(2,1)S(1)}, bf16[256,128]{1,0:T(8,128)(2,1)S(1)}, u32[]{:S(2)}, u32[]{:S(2)}) collective-permute-start(bf16[256,128]{1,0:T(8,128)(2,1)S(1)} %get-tuple-element.79), channel_id=1, source_target_pairs={{0,96},{16,112},{32,0},{48,16},{64,32},{80,48},{96,64},{112,80},{1... | collective-permute-start | bytes 196616 | tf_op jit(solution)/shard_map/ppermute | solution.py:236
  81.2 2.3 %collective-permute-done.14.far = bf16[1536,128]{1,0:T(8,128)(2,1)S(1)} collective-permute-done((bf16[1536,128]{1,0:T(8,128)(2,1)S(1)}, bf16[1536,128]{1,0:T(8,128)(2,1)S(1)}, u32[]{:S(2)}, u32[]{:S(2)}) %collective-permute-start.14) | collective-permute-done | bytes 393248 | tf_op jit(solution)/shard_map/ppermute | solution.py:246
  83.4 0.1 sum_prompt.1
  83.6 2.5 %collective-permute-start.15 = (bf16[384,128]{1,0:T(8,128)(2,1)S(1)}, bf16[384,128]{1,0:T(8,128)(2,1)S(1)}, u32[]{:S(2)}, u32[]{:S(2)}) collective-permute-start(bf16[384,128]{1,0:T(8,128)(2,1)S(1)} %get-tuple-element.74), channel_id=1, source_target_pairs={{0,96},{16,112},{32,0},{48,16},{64,32},{80,48},{96,64},{112,80},{1... | collective-permute-start | bytes 294920 | tf_op jit(solution)/shard_map/ppermute | solution.py:236
  86.1 2.5 %collective-permute-done.9.refs_1_ = bf16[256,512]{1,0:T(8,128)(2,1)S(1)} collective-permute-done((bf16[256,512]{1,0:T(8,128)(2,1)S(1)}, bf16[256,512]{1,0:T(8,128)(2,1)S(1)}, u32[]{:S(2)}, u32[]{:S(2)}) %collective-permute-start.9) | collective-permute-done | bytes 262176 | tf_op jit(solution)/shard_map/ppermute | solution.py:236
  88.6 0.8 collective-permute-start.16
  89.3 0.0 collective-permute-done.10.refs_2_
  89.3 3.9 %collective-permute-start.17 = (bf16[384,128]{1,0:T(8,128)(2,1)S(1)}, bf16[384,128]{1,0:T(8,128)(2,1)S(1)}, u32[]{:S(2)}, u32[]{:S(2)}) collective-permute-start(bf16[384,128]{1,0:T(8,128)(2,1)S(1)} %get-tuple-element.76), channel_id=1, source_target_pairs={{0,32},{16,48},{32,64},{48,80},{64,96},{80,112},{96,0},{112,16},{1... | collective-permute-start | bytes 294920 | tf_op jit(solution)/shard_map/ppermute | solution.py:236
  93.3 1.1 %collective-permute-start.19 = (bf16[256,128]{1,0:T(8,128)(2,1)S(1)}, bf16[256,128]{1,0:T(8,128)(2,1)S(1)}, u32[]{:S(2)}, u32[]{:S(2)}) collective-permute-start(bf16[256,128]{1,0:T(8,128)(2,1)S(1)} %get-tuple-element.80), channel_id=1, source_target_pairs={{0,64},{16,80},{32,96},{48,112},{64,0},{80,16},{96,32},{112,48},{1... | collective-permute-start | bytes 196616 | tf_op jit(solution)/shard_map/ppermute | solution.py:236
  94.4 0.6 copy-done.10
  95.0 1.6 %unpack_rows.1 = (bf16[128,2048]{1,0:T(8,128)(2,1)}, bf16[128,2048]{1,0:T(8,128)(2,1)}) custom-call(s32[3]{0:T(128)S(1)} %copy-done.10, bf16[256,512]{1,0:T(8,128)(2,1)S(1)} %copy-done.4, bf16[256,512]{1,0:T(8,128)(2,1)S(1)} %collective-permute-done.9.refs_1_, bf16[256,512]{1,0:T(8,128)(2,1)S(1)} %collective-permute-done.10.refs_2_, ...), custom_call_target="tpu_custom_call" | custom-call | tf_op jit(solution)/shard_map/unpack_rows/pallas_call | solution.py:334
  96.6 2.4 %collective-permute-done.19.refs_6_ = bf16[256,128]{1,0:T(8,128)(2,1)S(1)} collective-permute-done((bf16[256,128]{1,0:T(8,128)(2,1)S(1)}, bf16[256,128]{1,0:T(8,128)(2,1)S(1)}, u32[]{:S(2)}, u32[]{:S(2)}) %collective-permute-start.19) | collective-permute-done | bytes 65568 | tf_op jit(solution)/shard_map/ppermute | solution.py:236
  99.1 0.8 collective-permute-done.20.refs_7_
  99.9 1.5 %unpack_keys.1 = (bf16[192,512]{1,0:T(8,128)(2,1)}, bf16[192,512]{1,0:T(8,128)(2,1)}, bf16[128,512]{1,0:T(8,128)(2,1)}, bf16[128,512]{1,0:T(8,128)(2,1)}) custom-call(s32[3]{0:T(128)S(1)} %copy-done.10, bf16[384,128]{1,0:T(8,128)(2,1)S(1)} %get-tuple-element.73.refs_0_, bf16[384,128]{1,0:T(8,128)(2,1)S(1)} %collective-permute-done.15.refs_1_, ...), custom_call_target="tpu_custom_call" | custom-call | tf_op jit(solution)/shard_map/unpack_keys/pallas_call | solution.py:337
  (56 shorter events, 0.3 us)
Async XLA Ops:
  0.6 10.9 %copy-start.2 = (bf16[1,128,2048]{2,1,0:T(8,128)(2,1)S(1)}, bf16[1,128,2048]{2,1,0:T(8,128)(2,1)}, u32[]{:S(2)}) copy-start(bf16[1,128,2048]{2,1,0:T(8,128)(2,1)} %param.9) | copy-start | bytes 1572868
  1.4 10.1 %copy-start.9 = (s32[3]{0:T(128)}, s32[3]{0:T(128)S(1)}, u32[]{:S(2)}) copy-start(s32[3]{0:T(128)S(1)} %pad_add_fusion.place) | copy-start | bytes 40
  1.4 0.9 copy-start.5
  2.4 0.9 copy-start.6
  3.3 0.9 copy-start.7
  4.2 0.9 copy-start.8
  5.8 7.4 %collective-permute-start = (bf16[640,128]{1,0:T(8,128)(2,1)S(1)}, bf16[640,128]{1,0:T(8,128)(2,1)S(1)}, u32[]{:S(2)}, u32[]{:S(2)}) collective-permute-start(bf16[640,128]{1,0:T(8,128)(2,1)S(1)} %get-tuple-element.47), channel_id=1, source_target_pairs={{0,32},{16,48},{32,64},{48,80},{64,96},{80,112},{96,0},{112,16},{1... | collective-permute-start | bytes 491528 | tf_op jit(solution)/shard_map/ppermute | solution.py:236
  7.3 10.2 %collective-permute-start.1 = (bf16[640,128]{1,0:T(8,128)(2,1)S(1)}, bf16[640,128]{1,0:T(8,128)(2,1)S(1)}, u32[]{:S(2)}, u32[]{:S(2)}) collective-permute-start(bf16[640,128]{1,0:T(8,128)(2,1)S(1)} %get-tuple-element.48), channel_id=1, source_target_pairs={{0,64},{16,80},{32,96},{48,112},{64,0},{80,16},{96,32},{112,48},{1... | collective-permute-start | bytes 491528 | tf_op jit(solution)/shard_map/ppermute | solution.py:236
  10.1 7.5 %collective-permute-start.2 = (bf16[640,128]{1,0:T(8,128)(2,1)S(1)}, bf16[640,128]{1,0:T(8,128)(2,1)S(1)}, u32[]{:S(2)}, u32[]{:S(2)}) collective-permute-start(bf16[640,128]{1,0:T(8,128)(2,1)S(1)} %get-tuple-element.49), channel_id=1, source_target_pairs={{0,96},{16,112},{32,0},{48,16},{64,32},{80,48},{96,64},{112,80},{1... | collective-permute-start | bytes 491528 | tf_op jit(solution)/shard_map/ppermute | solution.py:236
  11.5 1.0 %copy-start.3 = (bf16[1,128,2048]{2,1,0:T(8,128)(2,1)S(1)}, bf16[1,128,2048]{2,1,0:T(8,128)(2,1)}, u32[]{:S(2)}) copy-start(bf16[1,128,2048]{2,1,0:T(8,128)(2,1)} %param.12) | copy-start | bytes 1572868
  13.2 0.7 copy-start.11
  17.6 15.0 %collective-permute-start.3 = (bf16[1536,128]{1,0:T(8,128)(2,1)S(1)}, bf16[1536,128]{1,0:T(8,128)(2,1)S(1)}, u32[]{:S(2)}, u32[]{:S(2)}) collective-permute-start(bf16[1536,128]{1,0:T(8,128)(2,1)S(1)} %pad_maximum_fusion), channel_id=1, source_target_pairs={{0,128},{128,0},{1,129},{129,1},{2,130},{130,2},{3,131},{131,3},{4... | collective-permute-start | bytes 1179656 | tf_op jit(solution)/shard_map/ppermute | solution.py:246
  18.0 9.3 %collective-permute-start.4 = (bf16[256,512]{1,0:T(8,128)(2,1)S(1)}, bf16[256,512]{1,0:T(8,128)(2,1)S(1)}, u32[]{:S(2)}, u32[]{:S(2)}) collective-permute-start(bf16[256,512]{1,0:T(8,128)(2,1)S(1)} %get-tuple-element.55), channel_id=1, source_target_pairs={{0,32},{16,48},{32,64},{48,80},{64,96},{80,112},{96,0},{112,16},{1... | collective-permute-start | bytes 786440 | tf_op jit(solution)/shard_map/ppermute | solution.py:236
  19.3 13.2 %collective-permute-start.5 = (bf16[256,512]{1,0:T(8,128)(2,1)S(1)}, bf16[256,512]{1,0:T(8,128)(2,1)S(1)}, u32[]{:S(2)}, u32[]{:S(2)}) collective-permute-start(bf16[256,512]{1,0:T(8,128)(2,1)S(1)} %get-tuple-element.56), channel_id=1, source_target_pairs={{0,64},{16,80},{32,96},{48,112},{64,0},{80,16},{96,32},{112,48},{1... | collective-permute-start | bytes 786440 | tf_op jit(solution)/shard_map/ppermute | solution.py:236
  21.7 10.9 %collective-permute-start.6 = (bf16[256,512]{1,0:T(8,128)(2,1)S(1)}, bf16[256,512]{1,0:T(8,128)(2,1)S(1)}, u32[]{:S(2)}, u32[]{:S(2)}) collective-permute-start(bf16[256,512]{1,0:T(8,128)(2,1)S(1)} %get-tuple-element.57), channel_id=1, source_target_pairs={{0,96},{16,112},{32,0},{48,16},{64,32},{80,48},{96,64},{112,80},{1... | collective-permute-start | bytes 786440 | tf_op jit(solution)/shard_map/ppermute | solution.py:236
  23.4 11.3 %copy-start.12 = (bf16[2560,128]{1,0:T(8,128)(2,1)}, bf16[2560,128]{1,0:T(8,128)(2,1)S(1)}, u32[]{:S(2)}) copy-start(bf16[2560,128]{1,0:T(8,128)(2,1)S(1)} %slice_dynamic-update-slice_fusion.refs_4_) | copy-start | bytes 1966084
  23.4 9.5 %collective-permute-start.7 = (bf16[2560,128]{1,0:T(8,128)(2,1)S(1)}, bf16[2560,128]{1,0:T(8,128)(2,1)S(1)}, u32[]{:S(2)}, u32[]{:S(2)}) collective-permute-start(bf16[2560,128]{1,0:T(8,128)(2,1)S(1)} %slice_dynamic-update-slice_fusion.refs_4_), channel_id=1, source_target_pairs={{0,16},{16,0},{32,48},{48,32},{64,80},{80,64},{96,112},{112,96},{1... | collective-permute-start | bytes 1966088 | tf_op jit(solution)/shard_map/ppermute | solution.py:242
  27.4 7.2 %copy-start.19 = (bf16[256,512]{1,0:T(8,128)(2,1)}, bf16[256,512]{1,0:T(8,128)(2,1)S(1)}, u32[]{:S(2)}) copy-start(bf16[256,512]{1,0:T(8,128)(2,1)S(1)} %collective-permute-done.4.refs_1_) | copy-start | bytes 786436
  32.6 2.0 %copy-start.20 = (bf16[256,512]{1,0:T(8,128)(2,1)}, bf16[256,512]{1,0:T(8,128)(2,1)S(1)}, u32[]{:S(2)}) copy-start(bf16[256,512]{1,0:T(8,128)(2,1)S(1)} %collective-permute-done.5.refs_2_) | copy-start | bytes 786436
  32.6 2.0 %copy-start.21 = (bf16[256,512]{1,0:T(8,128)(2,1)}, bf16[256,512]{1,0:T(8,128)(2,1)S(1)}, u32[]{:S(2)}) copy-start(bf16[256,512]{1,0:T(8,128)(2,1)S(1)} %collective-permute-done.6.refs_3_) | copy-start | bytes 786436
  32.6 2.0 %copy-start.14 = (bf16[1536,128]{1,0:T(8,128)(2,1)}, bf16[1536,128]{1,0:T(8,128)(2,1)S(1)}, u32[]{:S(2)}) copy-start(bf16[1536,128]{1,0:T(8,128)(2,1)S(1)} %collective-permute-done.3.refs_6_) | copy-start | bytes 1179652
  32.6 2.0 %collective-permute-start.8 = (bf16[1536,128]{1,0:T(8,128)(2,1)S(1)}, bf16[1536,128]{1,0:T(8,128)(2,1)S(1)}, u32[]{:S(2)}, u32[]{:S(2)}) collective-permute-start(bf16[1536,128]{1,0:T(8,128)(2,1)S(1)} %collective-permute-done.3.refs_6_), channel_id=1, source_target_pairs={{0,16},{16,0},{32,48},{48,32},{64,80},{80,64},{96,112},{112,96},{1... | collective-permute-start | bytes 1179656 | tf_op jit(solution)/shard_map/ppermute | solution.py:242
  32.9 1.7 %copy-start.13 = (bf16[2560,128]{1,0:T(8,128)(2,1)}, bf16[2560,128]{1,0:T(8,128)(2,1)S(1)}, u32[]{:S(2)}) copy-start(bf16[2560,128]{1,0:T(8,128)(2,1)S(1)} %collective-permute-done.7.refs_5_) | copy-start | bytes 1966084
  34.6 0.8 copy-start.15
  67.4 1.9 %collective-permute-start.13 = (bf16[1536,128]{1,0:T(8,128)(2,1)}, bf16[1536,128]{1,0:T(8,128)(2,1)S(1)}, u32[]{:S(2)}, u32[]{:S(2)}) collective-permute-start(bf16[1536,128]{1,0:T(8,128)(2,1)} %get-tuple-element.72), channel_id=1, source_target_pairs={{0,16},{16,0},{32,48},{48,32},{64,80},{80,64},{96,112},{112,96},{1... | collective-permute-start | bytes 1179656 | tf_op jit(solution)/shard_map/ppermute | solution.py:242
  67.5 10.0 %collective-permute-start.12 = (bf16[2560,128]{1,0:T(8,128)(2,1)}, bf16[2560,128]{1,0:T(8,128)(2,1)S(1)}, u32[]{:S(2)}, u32[]{:S(2)}) collective-permute-start(bf16[2560,128]{1,0:T(8,128)(2,1)} %get-tuple-element.70), channel_id=1, source_target_pairs={{0,16},{16,0},{32,48},{48,32},{64,80},{80,64},{96,112},{112,96},{1... | collective-permute-start | bytes 1966088 | tf_op jit(solution)/shard_map/ppermute | solution.py:242
  69.4 4.6 %copy-start.18 = (bf16[256,512]{1,0:T(8,128)(2,1)S(1)}, bf16[256,512]{1,0:T(8,128)(2,1)}, u32[]{:S(2)}) copy-start(bf16[256,512]{1,0:T(8,128)(2,1)} %get-tuple-element.64) | copy-start | bytes 786436
  69.4 7.0 %copy-start.17 = (bf16[256,512]{1,0:T(8,128)(2,1)S(1)}, bf16[256,512]{1,0:T(8,128)(2,1)}, u32[]{:S(2)}) copy-start(bf16[256,512]{1,0:T(8,128)(2,1)} %get-tuple-element.65) | copy-start | bytes 786436
  69.4 8.2 %copy-start.16 = (bf16[256,512]{1,0:T(8,128)(2,1)S(1)}, bf16[256,512]{1,0:T(8,128)(2,1)}, u32[]{:S(2)}) copy-start(bf16[256,512]{1,0:T(8,128)(2,1)} %get-tuple-element.66) | copy-start | bytes 786436
  69.4 8.2 %copy-start.1 = (f32[1024,128]{1,0:T(8,128)S(1)}, f32[1024,128]{1,0:T(8,128)}, u32[]{:S(2)}) copy-start(f32[1024,128]{1,0:T(8,128)} %get-tuple-element.77.own) | copy-start | bytes 1572868
  70.7 12.8 %copy-start = (f32[1536,128]{1,0:T(8,128)S(1)}, f32[1536,128]{1,0:T(8,128)}, u32[]{:S(2)}) copy-start(f32[1536,128]{1,0:T(8,128)} %get-tuple-element.69.own) | copy-start | bytes 2359300
  70.7 12.7 %collective-permute-start.14 = (bf16[1536,128]{1,0:T(8,128)(2,1)S(1)}, bf16[1536,128]{1,0:T(8,128)(2,1)S(1)}, u32[]{:S(2)}, u32[]{:S(2)}) collective-permute-start(bf16[1536,128]{1,0:T(8,128)(2,1)S(1)} %add_convert_fusion), channel_id=1, source_target_pairs={{0,128},{128,0},{1,129},{129,1},{2,130},{130,2},{3,131},{131,3},{4... | collective-permute-start | bytes 1179656 | tf_op jit(solution)/shard_map/ppermute | solution.py:246
  73.9 14.6 %collective-permute-start.9 = (bf16[256,512]{1,0:T(8,128)(2,1)S(1)}, bf16[256,512]{1,0:T(8,128)(2,1)S(1)}, u32[]{:S(2)}, u32[]{:S(2)}) collective-permute-start(bf16[256,512]{1,0:T(8,128)(2,1)S(1)} %copy-done.18), channel_id=1, source_target_pairs={{0,96},{16,112},{32,0},{48,16},{64,32},{80,48},{96,64},{112,80},{1... | collective-permute-start | bytes 786440 | tf_op jit(solution)/shard_map/ppermute | solution.py:236
  76.4 12.9 %collective-permute-start.10 = (bf16[256,512]{1,0:T(8,128)(2,1)S(1)}, bf16[256,512]{1,0:T(8,128)(2,1)S(1)}, u32[]{:S(2)}, u32[]{:S(2)}) collective-permute-start(bf16[256,512]{1,0:T(8,128)(2,1)S(1)} %copy-done.17), channel_id=1, source_target_pairs={{0,64},{16,80},{32,96},{48,112},{64,0},{80,16},{96,32},{112,48},{1... | collective-permute-start | bytes 786440 | tf_op jit(solution)/shard_map/ppermute | solution.py:236
  77.6 15.7 %collective-permute-start.11 = (bf16[256,512]{1,0:T(8,128)(2,1)S(1)}, bf16[256,512]{1,0:T(8,128)(2,1)S(1)}, u32[]{:S(2)}, u32[]{:S(2)}) collective-permute-start(bf16[256,512]{1,0:T(8,128)(2,1)S(1)} %copy-done.16), channel_id=1, source_target_pairs={{0,32},{16,48},{32,64},{48,80},{64,96},{80,112},{96,0},{112,16},{1... | collective-permute-start | bytes 786440 | tf_op jit(solution)/shard_map/ppermute | solution.py:236
  77.6 16.7 %collective-permute-start.18 = (bf16[256,128]{1,0:T(8,128)(2,1)S(1)}, bf16[256,128]{1,0:T(8,128)(2,1)S(1)}, u32[]{:S(2)}, u32[]{:S(2)}) collective-permute-start(bf16[256,128]{1,0:T(8,128)(2,1)S(1)} %get-tuple-element.79), channel_id=1, source_target_pairs={{0,96},{16,112},{32,0},{48,16},{64,32},{80,48},{96,64},{112,80},{1... | collective-permute-start | bytes 196616 | tf_op jit(solution)/shard_map/ppermute | solution.py:236
  83.4 10.9 %copy-start.4 = (bf16[256,512]{1,0:T(8,128)(2,1)S(1)}, bf16[256,512]{1,0:T(8,128)(2,1)}, u32[]{:S(2)}) copy-start(bf16[256,512]{1,0:T(8,128)(2,1)} %get-tuple-element.63.refs_0_) | copy-start | bytes 786436
  83.6 16.3 %collective-permute-start.15 = (bf16[384,128]{1,0:T(8,128)(2,1)S(1)}, bf16[384,128]{1,0:T(8,128)(2,1)S(1)}, u32[]{:S(2)}, u32[]{:S(2)}) collective-permute-start(bf16[384,128]{1,0:T(8,128)(2,1)S(1)} %get-tuple-element.74), channel_id=1, source_target_pairs={{0,96},{16,112},{32,0},{48,16},{64,32},{80,48},{96,64},{112,80},{1... | collective-permute-start | bytes 294920 | tf_op jit(solution)/shard_map/ppermute | solution.py:236
  88.6 11.3 %collective-permute-start.16 = (bf16[384,128]{1,0:T(8,128)(2,1)S(1)}, bf16[384,128]{1,0:T(8,128)(2,1)S(1)}, u32[]{:S(2)}, u32[]{:S(2)}) collective-permute-start(bf16[384,128]{1,0:T(8,128)(2,1)S(1)} %get-tuple-element.75), channel_id=1, source_target_pairs={{0,64},{16,80},{32,96},{48,112},{64,0},{80,16},{96,32},{112,48},{1... | collective-permute-start | bytes 294920 | tf_op jit(solution)/shard_map/ppermute | solution.py:236
  89.3 10.5 %collective-permute-start.17 = (bf16[384,128]{1,0:T(8,128)(2,1)S(1)}, bf16[384,128]{1,0:T(8,128)(2,1)S(1)}, u32[]{:S(2)}, u32[]{:S(2)}) collective-permute-start(bf16[384,128]{1,0:T(8,128)(2,1)S(1)} %get-tuple-element.76), channel_id=1, source_target_pairs={{0,32},{16,48},{32,64},{48,80},{64,96},{80,112},{96,0},{112,16},{1... | collective-permute-start | bytes 294920 | tf_op jit(solution)/shard_map/ppermute | solution.py:236
  93.3 5.8 %collective-permute-start.19 = (bf16[256,128]{1,0:T(8,128)(2,1)S(1)}, bf16[256,128]{1,0:T(8,128)(2,1)S(1)}, u32[]{:S(2)}, u32[]{:S(2)}) collective-permute-start(bf16[256,128]{1,0:T(8,128)(2,1)S(1)} %get-tuple-element.80), channel_id=1, source_target_pairs={{0,64},{16,80},{32,96},{48,112},{64,0},{80,16},{96,32},{112,48},{1... | collective-permute-start | bytes 196616 | tf_op jit(solution)/shard_map/ppermute | solution.py:236
  94.4 0.7 copy-start.10
  94.4 5.5 %collective-permute-start.20 = (bf16[256,128]{1,0:T(8,128)(2,1)S(1)}, bf16[256,128]{1,0:T(8,128)(2,1)S(1)}, u32[]{:S(2)}, u32[]{:S(2)}) collective-permute-start(bf16[256,128]{1,0:T(8,128)(2,1)S(1)} %get-tuple-element.81), channel_id=1, source_target_pairs={{0,32},{16,48},{32,64},{48,80},{64,96},{80,112},{96,0},{112,16},{1... | collective-permute-start | bytes 196616 | tf_op jit(solution)/shard_map/ppermute | solution.py:236
where the time goes:
time: 102 us; the launch traced here: 101 us
  Pallas kernels  36.5 us (36%)
  starting transfers between devices  31 us (30%)
  waiting for transfers between devices  23.9 us (23%)
  local copies, waits for them, and re-layouts  6.94 us (7%)
  between operations  1.61 us (2%)
  other arithmetic  1.42 us (1%)
    pallas_call x1, Pallas kernels, per_device(): pl.pallas_call(attention, out_shape=[rows] * 4 + [shape(far_block, F32),...  32 us
    ppermute x15, starting transfers between devices, to_chip(): lax.ppermute(a, 'ctx', [(2 * x + c, 2 * ((x + d) % CHIPS) + c) for x in r...  26.5 us
    ppermute x15, waiting for transfers between devices, to_chip(): lax.ppermute(a, 'ctx', [(2 * x + c, 2 * ((x + d) % CHIPS) + c) for x in r...  18.5 us
    unnamed x51, local copies, waits for them, and re-layouts  6.93 us
    ppermute x2, starting transfers between devices, to_pair(): return lax.ppermute(a, 'pair', [(0, 1), (1, 0)])  3.66 us
    ppermute x4, waiting for transfers between devices, to_core(): return lax.ppermute(a, 'ctx', [(i, i ^ 1) for i in range(2 * CHIPS)])  3.12 us
    ppermute x2, waiting for transfers between devices, to_pair(): return lax.ppermute(a, 'pair', [(0, 1), (1, 0)])  2.26 us
  transfers between devices with their start and end apart: 21, of which 9 were waited for; matrix products, arithmetic and copies ran while one was open for 1% of the time, Pallas kernels for 2%

commit v1 on v0

--- a/solution.py
+++ b/solution.py
@@ -33,14 +33,22 @@
     return pl.ds(pl.multiple_of(index * width, width), width)
 
 
-def pack_keys(place, pk, pv, rk, rv, *outs):
+def pack_keys(place, pk, pv, rk, rv, *refs):
     x = place[2]
+    sems = refs[4]
+    copies = []
     for d in range(CHIPS):
         head = lanes(lax.rem(x + d, CHIPS), 128)
-        outs[d][0:192, :] = pk[:, head]
-        outs[d][192:384, :] = pv[:, head]
-        outs[d][384:512, :] = rk[:, head]
-        outs[d][512:640, :] = rv[:, head]
+        for src, lo, hi in ((pk, 0, 192), (pv, 192, 384), (rk, 384, 512), (rv, 512, 640)):
+            copies.append(
+                pltpu.make_async_copy(
+                    src.at[:, head], refs[d].at[lo:hi, :], sems.at[len(copies)]
+                )
+            )
+    for copy in copies:
+        copy.start()
+    for copy in copies:
+        copy.wait()
 
 
 def pack_rows(place, q, g, *outs):
@@ -91,7 +99,7 @@
     oq_out = refs[8:12]
     own_out, resp_out, other_out = refs[12:15]
     dprompt_out = (own_out, other_out, refs[15], refs[16])
-    (qs, gs, os_, qn, qT, gT, gn, kk, kT, vv, vT, sp, ee, ds_s, dq, dkp, dvp, dkr, dvr) = refs[17:]
+    (qs, gs, os_, qn, qT, gT, gn, kk, kT, vv, vT, sp, ee, dq, dkp, dvp, dkr, dvr) = refs[17:]
     c, length, x = place[0], place[1], place[2]
 
     chip_of = [lax.rem(x + CHIPS - d, CHIPS) for d in range(CHIPS)]
@@ -181,10 +189,10 @@
     def prompt_block(t, _):
         keys = pl.ds(pl.multiple_of(t * KEY_BLOCK, KEY_BLOCK), KEY_BLOCK)
         dp = dot(vv[keys, :], gT[...])
-        ds_s[...] = (dp * ee[keys, :].astype(F32)).astype(BF)
         dvp[keys, :] = dot(ee[keys, :], gn[...])
-        dkp[keys, :] = dot(ds_s[...], qn[...]) * SCALE
-        part = dot(kT[:, keys], ds_s[...])
+        ee[keys, :] = (dp * ee[keys, :].astype(F32)).astype(BF)
+        dkp[keys, :] = dot(ee[keys, :], qn[...]) * SCALE
+        part = dot(kT[:, keys], ee[keys, :])
 
         @pl.when(t == 0)
         def _():
@@ -269,11 +277,18 @@
     far_block = (1536, 128)
     own_block = (2560, 128)
 
-    packed = small(pack_keys, "pack_keys", [block] * 4, 4)(
-        place, prompt_keys, prompt_values, resp_keys[0], resp_values[0]
-    )
-    kv = spread(packed, 1)
+    kv = pl.pallas_call(
+        pack_keys,
+        out_shape=[block] * 4,
+        in_specs=[SMEM] + [pl.BlockSpec(memory_space=pltpu.HBM)] * 4,
+        out_specs=[VMEM] * 4,
+        scratch_shapes=[pltpu.SemaphoreType.DMA((16,))],
+        name="pack_keys",
+    )(place, prompt_keys, prompt_values, resp_keys[0], resp_values[0])
+    kv = spread(kv, 1)
     packed = small(pack_rows, "pack_rows", [rows] * 4, 2)(place, resp_queries[0], out_grad[0])
+    held = lax.optimization_barrier(tuple(packed) + tuple(kv))
+    packed, kv = held[:4], held[4:]
     prompt = jnp.concatenate([k[:384] for k in kv], axis=0)
     own = jnp.concatenate([k[:384] for k in kv] + [k[384:] for k in kv], axis=0)
     far = to_pair(prompt)
@@ -306,14 +321,13 @@
             pltpu.VMEM((144, KEYS), BF),
             pltpu.VMEM((2, KEYS, 512), F32),
             pltpu.VMEM((KEYS, all_rows), BF),
-            pltpu.VMEM((KEY_BLOCK, all_rows), BF),
             pltpu.VMEM((128, all_rows), F32),
             pltpu.VMEM((PROMPT_KEYS, 128), F32),
             pltpu.VMEM((PROMPT_KEYS, 128), F32),
             pltpu.VMEM((1024, 128), F32),
             pltpu.VMEM((1024, 128), F32),
         ],
-        compiler_params=pltpu.CompilerParams(vmem_limit_bytes=60 << 20),
+        compiler_params=pltpu.CompilerParams(vmem_limit_bytes=50 << 20),
         cost_estimate=pl.CostEstimate(
             flops=10 * 2048 * 3712 * 128, bytes_accessed=10 << 20, transcendentals=2048 * 3712
         ),

time: 102 us -> 98.3 us (0.964)
  local copies, waits for them, and re-layouts: 6.94 us -> 1.8 us
    unnamed x51 -> x21, local copies, waits for them, and re-layouts: 6.93 us -> 1.79 us
    pallas_call x1, Pallas kernels: 0.67 us -> 2.72 us  [per_device(): pl.pallas_call(pack_keys, out_shape=[block] * 4, in_specs=[SMEM] + [pl.Bl...]
    pallas_call x1, Pallas kernels: 32 us -> 30.9 us  [per_device(): pl.pallas_call(attention, out_shape=[rows] * 4 + [shape(far_block, F32),...]
where the time goes in v1:
time: 98.3 us; the launch traced here: 98 us
  Pallas kernels  37.5 us (38%)
  starting transfers between devices  30.4 us (31%)
  waiting for transfers between devices  24.9 us (25%)
  other arithmetic  1.82 us (2%)
  local copies, waits for them, and re-layouts  1.8 us (2%)
  between operations  1.51 us (2%)
    pallas_call x1, Pallas kernels, per_device(): pl.pallas_call(attention, out_shape=[rows] * 4 + [shape(far_block, F32),...  30.9 us
    ppermute x15, starting transfers between devices, to_chip(): lax.ppermute(a, 'ctx', [(2 * x + c, 2 * ((x + d) % CHIPS) + c) for x in r...  26.1 us
    ppermute x15, waiting for transfers between devices, to_chip(): lax.ppermute(a, 'ctx', [(2 * x + c, 2 * ((x + d) % CHIPS) + c) for x in r...  19.5 us
    ppermute x2, starting transfers between devices, to_pair(): return lax.ppermute(a, 'pair', [(0, 1), (1, 0)])  3.66 us
    ppermute x4, waiting for transfers between devices, to_core(): return lax.ppermute(a, 'ctx', [(i, i ^ 1) for i in range(2 * CHIPS)])  2.91 us
    pallas_call x1, Pallas kernels, per_device(): pl.pallas_call(pack_keys, out_shape=[block] * 4, in_specs=[SMEM] + [pl.Bl...  2.72 us
    ppermute x2, waiting for transfers between devices, to_pair(): return lax.ppermute(a, 'pair', [(0, 1), (1, 0)])  2.56 us
  transfers between devices with their start and end apart: 21, of which 9 were waited for; matrix products, arithmetic and copies ran while one was open for 1% of the time, Pallas kernels for 2%

profile of v1, /device:TPU:112, one launch (start us, length us, event | category | flops | bytes accessed | tf_op | source)
XLA Modules:
  0.0 98.0 jit_solution(1941391725555796950)
XLA Ops:
  1.4 0.6 pad_add_fusion.place
  1.9 2.7 %pack_keys.1 = (bf16[640,128]{1,0:T(8,128)(2,1)}, bf16[640,128]{1,0:T(8,128)(2,1)}, bf16[640,128]{1,0:T(8,128)(2,1)}, bf16[640,128]{1,0:T(8,128)(2,1)}) custom-call(s32[3]{0:T(128)} %pad_add_fusion.place, bf16[192,512]{1,0:T(8,128)(2,1)} %pk.1, bf16[192,512]{1,0:T(8,128)(2,1)} %pv.1, bf16[128,512]{1,0:T(8,128)(2,1)} %bitcast.12, bf16[128,512]{1,0:T(8,128)(2,1)} %bitcast.13), custom_call_target="tpu_custom_call" | custom-call | tf_op jit(solution)/shard_map/pack_keys/pallas_call | solution.py:280
  4.7 1.6 %collective-permute-start = (bf16[640,128]{1,0:T(8,128)(2,1)}, bf16[640,128]{1,0:T(8,128)(2,1)S(1)}, u32[]{:S(2)}, u32[]{:S(2)}) collective-permute-start(bf16[640,128]{1,0:T(8,128)(2,1)} %get-tuple-element.59), channel_id=1, source_target_pairs={{0,32},{16,48},{32,64},{48,80},{64,96},{80,112},{96,0},{112,16},{1... | collective-permute-start | bytes 491528 | tf_op jit(solution)/shard_map/ppermute | solution.py:244
  6.2 2.7 %collective-permute-start.1 = (bf16[640,128]{1,0:T(8,128)(2,1)}, bf16[640,128]{1,0:T(8,128)(2,1)S(1)}, u32[]{:S(2)}, u32[]{:S(2)}) collective-permute-start(bf16[640,128]{1,0:T(8,128)(2,1)} %get-tuple-element.60), channel_id=1, source_target_pairs={{0,64},{16,80},{32,96},{48,112},{64,0},{80,16},{96,32},{112,48},{1... | collective-permute-start | bytes 491528 | tf_op jit(solution)/shard_map/ppermute | solution.py:244
  9.0 1.4 %collective-permute-start.2 = (bf16[640,128]{1,0:T(8,128)(2,1)}, bf16[640,128]{1,0:T(8,128)(2,1)S(1)}, u32[]{:S(2)}, u32[]{:S(2)}) collective-permute-start(bf16[640,128]{1,0:T(8,128)(2,1)} %get-tuple-element.61), channel_id=1, source_target_pairs={{0,96},{16,112},{32,0},{48,16},{64,32},{80,48},{96,64},{112,80},{1... | collective-permute-start | bytes 491528 | tf_op jit(solution)/shard_map/ppermute | solution.py:244
  10.4 0.6 copy-done.3
  11.0 1.0 %copy-done.2 = bf16[1,128,2048]{2,1,0:T(8,128)(2,1)S(1)} copy-done((bf16[1,128,2048]{2,1,0:T(8,128)(2,1)S(1)}, bf16[1,128,2048]{2,1,0:T(8,128)(2,1)}, u32[]{:S(2)}) %copy-start.2) | copy-done | bytes 524312
  12.0 0.6 pack_rows.1
  12.7 0.0 collective-permute-done
  12.7 3.9 %collective-permute-done.1 = bf16[640,128]{1,0:T(8,128)(2,1)S(1)} collective-permute-done((bf16[640,128]{1,0:T(8,128)(2,1)}, bf16[640,128]{1,0:T(8,128)(2,1)S(1)}, u32[]{:S(2)}, u32[]{:S(2)}) %collective-permute-start.1) | collective-permute-done | bytes 163872 | tf_op jit(solution)/shard_map/ppermute | solution.py:244
  16.6 0.0 collective-permute-done.2
  16.8 0.4 collective-permute-start.3
  17.2 1.3 %collective-permute-start.4 = (bf16[256,512]{1,0:T(8,128)(2,1)S(1)}, bf16[256,512]{1,0:T(8,128)(2,1)S(1)}, u32[]{:S(2)}, u32[]{:S(2)}) collective-permute-start(bf16[256,512]{1,0:T(8,128)(2,1)S(1)} %get-tuple-element.71), channel_id=1, source_target_pairs={{0,32},{16,48},{32,64},{48,80},{64,96},{80,112},{96,0},{112,16},{1... | collective-permute-start | bytes 786440 | tf_op jit(solution)/shard_map/ppermute | solution.py:244
  18.6 2.4 %collective-permute-start.5 = (bf16[256,512]{1,0:T(8,128)(2,1)S(1)}, bf16[256,512]{1,0:T(8,128)(2,1)S(1)}, u32[]{:S(2)}, u32[]{:S(2)}) collective-permute-start(bf16[256,512]{1,0:T(8,128)(2,1)S(1)} %get-tuple-element.72), channel_id=1, source_target_pairs={{0,64},{16,80},{32,96},{48,112},{64,0},{80,16},{96,32},{112,48},{1... | collective-permute-start | bytes 786440 | tf_op jit(solution)/shard_map/ppermute | solution.py:244
  21.0 1.6 %collective-permute-start.6 = (bf16[256,512]{1,0:T(8,128)(2,1)S(1)}, bf16[256,512]{1,0:T(8,128)(2,1)S(1)}, u32[]{:S(2)}, u32[]{:S(2)}) collective-permute-start(bf16[256,512]{1,0:T(8,128)(2,1)S(1)} %get-tuple-element.73), channel_id=1, source_target_pairs={{0,96},{16,112},{32,0},{48,16},{64,32},{80,48},{96,64},{112,80},{1... | collective-permute-start | bytes 786440 | tf_op jit(solution)/shard_map/ppermute | solution.py:244
  22.5 0.1 collective-permute-start.7
  22.6 3.9 %collective-permute-done.4.refs_1_ = bf16[256,512]{1,0:T(8,128)(2,1)S(1)} collective-permute-done((bf16[256,512]{1,0:T(8,128)(2,1)S(1)}, bf16[256,512]{1,0:T(8,128)(2,1)S(1)}, u32[]{:S(2)}, u32[]{:S(2)}) %collective-permute-start.4) | collective-permute-done | bytes 262176 | tf_op jit(solution)/shard_map/ppermute | solution.py:244
  26.5 5.3 %collective-permute-done.5.refs_2_ = bf16[256,512]{1,0:T(8,128)(2,1)S(1)} collective-permute-done((bf16[256,512]{1,0:T(8,128)(2,1)S(1)}, bf16[256,512]{1,0:T(8,128)(2,1)S(1)}, u32[]{:S(2)}, u32[]{:S(2)}) %collective-permute-start.5) | collective-permute-done | bytes 262176 | tf_op jit(solution)/shard_map/ppermute | solution.py:244
  31.8 0.0 collective-permute-done.6.refs_3_
  31.8 0.0 collective-permute-done.3.refs_6_
  31.8 0.0 collective-permute-start.8
  31.8 0.0 collective-permute-done.7.refs_5_
  31.9 1.7 %collective-permute-done.8.refs_7_ = bf16[1536,128]{1,0:T(8,128)(2,1)S(1)} collective-permute-done((bf16[1536,128]{1,0:T(8,128)(2,1)S(1)}, bf16[1536,128]{1,0:T(8,128)(2,1)S(1)}, u32[]{:S(2)}, u32[]{:S(2)}) %collective-permute-start.8) | collective-permute-done | bytes 393248 | tf_op jit(solution)/shard_map/ppermute | solution.py:250
  33.6 30.9 %attention.1 = (bf16[256,512]{1,0:T(8,128)(2,1)S(1)}, bf16[256,512]{1,0:T(8,128)(2,1)S(1)}, bf16[256,512]{1,0:T(8,128)(2,1)S(1)}, bf16[256,512]{1,0:T(8,128)(2,1...) custom-call(s32[3]{0:T(128)S(1)} %copy-done.3, ...), custom_call_target="tpu_custom_call" | custom-call | flops 9730785280 | bytes 10485760 | tf_op jit(solution)/shard_map/attention/pallas_call | solution.py:303
  64.4 0.1 collective-permute-start.13
  64.6 0.4 collective-permute-start.12
  64.9 1.2 %collective-permute-done.13 = bf16[1536,128]{1,0:T(8,128)(2,1)S(1)} collective-permute-done((bf16[1536,128]{1,0:T(8,128)(2,1)S(1)}, bf16[1536,128]{1,0:T(8,128)(2,1)S(1)}, u32[]{:S(2)}, u32[]{:S(2)}) %collective-permute-start.13) | collective-permute-done | bytes 393248 | tf_op jit(solution)/shard_map/ppermute | solution.py:250
  66.1 1.2 %add_convert_fusion = bf16[1536,128]{1,0:T(8,128)(2,1)S(1)} fusion(f32[1536,128]{1,0:T(8,128)} %get-tuple-element.87, bf16[1536,128]{1,0:T(8,128)(2,1)S(1)} %collective-permute-done.13), kind=kLoop, calls=%fused_computation | loop fusion | flops 589824 | bytes 1572864 | tf_op jit(solution)/shard_map/convert_element_type | solution.py:342
  67.4 3.2 %collective-permute-start.14 = (bf16[1536,128]{1,0:T(8,128)(2,1)S(1)}, bf16[1536,128]{1,0:T(8,128)(2,1)S(1)}, u32[]{:S(2)}, u32[]{:S(2)}) collective-permute-start(bf16[1536,128]{1,0:T(8,128)(2,1)S(1)} %add_convert_fusion), channel_id=1, source_target_pairs={{0,128},{128,0},{1,129},{129,1},{2,130},{130,2},{3,131},{131,3},{4... | collective-permute-start | bytes 1179656 | tf_op jit(solution)/shard_map/ppermute | solution.py:254
  70.6 2.4 %collective-permute-start.9 = (bf16[256,512]{1,0:T(8,128)(2,1)S(1)}, bf16[256,512]{1,0:T(8,128)(2,1)S(1)}, u32[]{:S(2)}, u32[]{:S(2)}) collective-permute-start(bf16[256,512]{1,0:T(8,128)(2,1)S(1)} %get-tuple-element.80), channel_id=1, source_target_pairs={{0,96},{16,112},{32,0},{48,16},{64,32},{80,48},{96,64},{112,80},{1... | collective-permute-start | bytes 786440 | tf_op jit(solution)/shard_map/ppermute | solution.py:244
  73.0 1.1 %collective-permute-start.10 = (bf16[256,512]{1,0:T(8,128)(2,1)S(1)}, bf16[256,512]{1,0:T(8,128)(2,1)S(1)}, u32[]{:S(2)}, u32[]{:S(2)}) collective-permute-start(bf16[256,512]{1,0:T(8,128)(2,1)S(1)} %get-tuple-element.81), channel_id=1, source_target_pairs={{0,64},{16,80},{32,96},{48,112},{64,0},{80,16},{96,32},{112,48},{1... | collective-permute-start | bytes 786440 | tf_op jit(solution)/shard_map/ppermute | solution.py:244
  74.2 0.0 collective-permute-start.11
  74.2 0.0 collective-permute-done.12.other
  74.2 0.1 sum_resp.1
  74.3 3.3 %collective-permute-start.18 = (bf16[256,128]{1,0:T(8,128)(2,1)S(1)}, bf16[256,128]{1,0:T(8,128)(2,1)S(1)}, u32[]{:S(2)}, u32[]{:S(2)}) collective-permute-start(bf16[256,128]{1,0:T(8,128)(2,1)S(1)} %get-tuple-element.95), channel_id=1, source_target_pairs={{0,96},{16,112},{32,0},{48,16},{64,32},{80,48},{96,64},{112,80},{1... | collective-permute-start | bytes 196616 | tf_op jit(solution)/shard_map/ppermute | solution.py:244
  77.6 2.6 %collective-permute-done.14.far = bf16[1536,128]{1,0:T(8,128)(2,1)S(1)} collective-permute-done((bf16[1536,128]{1,0:T(8,128)(2,1)S(1)}, bf16[1536,128]{1,0:T(8,128)(2,1)S(1)}, u32[]{:S(2)}, u32[]{:S(2)}) %collective-permute-start.14) | collective-permute-done | bytes 393248 | tf_op jit(solution)/shard_map/ppermute | solution.py:254
  80.1 0.1 sum_prompt.1
  80.2 2.5 %collective-permute-start.15 = (bf16[384,128]{1,0:T(8,128)(2,1)S(1)}, bf16[384,128]{1,0:T(8,128)(2,1)S(1)}, u32[]{:S(2)}, u32[]{:S(2)}) collective-permute-start(bf16[384,128]{1,0:T(8,128)(2,1)S(1)} %get-tuple-element.90), channel_id=1, source_target_pairs={{0,96},{16,112},{32,0},{48,16},{64,32},{80,48},{96,64},{112,80},{1... | collective-permute-start | bytes 294920 | tf_op jit(solution)/shard_map/ppermute | solution.py:244
  82.7 2.5 %collective-permute-done.9.refs_1_ = bf16[256,512]{1,0:T(8,128)(2,1)S(1)} collective-permute-done((bf16[256,512]{1,0:T(8,128)(2,1)S(1)}, bf16[256,512]{1,0:T(8,128)(2,1)S(1)}, u32[]{:S(2)}, u32[]{:S(2)}) %collective-permute-start.9) | collective-permute-done | bytes 262176 | tf_op jit(solution)/shard_map/ppermute | solution.py:244
  85.2 0.7 collective-permute-start.16
  85.9 0.0 collective-permute-done.10.refs_2_
  85.9 4.0 %collective-permute-start.17 = (bf16[384,128]{1,0:T(8,128)(2,1)S(1)}, bf16[384,128]{1,0:T(8,128)(2,1)S(1)}, u32[]{:S(2)}, u32[]{:S(2)}) collective-permute-start(bf16[384,128]{1,0:T(8,128)(2,1)S(1)} %get-tuple-element.92), channel_id=1, source_target_pairs={{0,32},{16,48},{32,64},{48,80},{64,96},{80,112},{96,0},{112,16},{1... | collective-permute-start | bytes 294920 | tf_op jit(solution)/shard_map/ppermute | solution.py:244
  89.9 1.0 %collective-permute-start.19 = (bf16[256,128]{1,0:T(8,128)(2,1)S(1)}, bf16[256,128]{1,0:T(8,128)(2,1)S(1)}, u32[]{:S(2)}, u32[]{:S(2)}) collective-permute-start(bf16[256,128]{1,0:T(8,128)(2,1)S(1)} %get-tuple-element.96), channel_id=1, source_target_pairs={{0,64},{16,80},{32,96},{48,112},{64,0},{80,16},{96,32},{112,48},{1... | collective-permute-start | bytes 196616 | tf_op jit(solution)/shard_map/ppermute | solution.py:244
  91.0 1.6 %unpack_rows.1 = (bf16[128,2048]{1,0:T(8,128)(2,1)}, bf16[128,2048]{1,0:T(8,128)(2,1)}) custom-call(s32[3]{0:T(128)S(1)} %copy-done.3, bf16[256,512]{1,0:T(8,128)(2,1)S(1)} %get-tuple-element.79.refs_0_, bf16[256,512]{1,0:T(8,128)(2,1)S(1)} %collective-permute-done.9.refs_1_, bf16[256,512]{1,0:T(8,128)(2,1)S(1)} %collective-permute-done.10.refs_2_, ...), custom_call_target="tpu_custom_call" | custom-call | tf_op jit(solution)/shard_map/unpack_rows/pallas_call | solution.py:348
  92.5 3.2 %collective-permute-done.19.refs_6_ = bf16[256,128]{1,0:T(8,128)(2,1)S(1)} collective-permute-done((bf16[256,128]{1,0:T(8,128)(2,1)S(1)}, bf16[256,128]{1,0:T(8,128)(2,1)S(1)}, u32[]{:S(2)}, u32[]{:S(2)}) %collective-permute-start.19) | collective-permute-done | bytes 65568 | tf_op jit(solution)/shard_map/ppermute | solution.py:244
  95.7 0.7 collective-permute-done.20.refs_7_
  96.4 0.0 collective-permute-done.15.refs_1_
  96.4 1.5 %unpack_keys.1 = (bf16[192,512]{1,0:T(8,128)(2,1)}, bf16[192,512]{1,0:T(8,128)(2,1)}, bf16[128,512]{1,0:T(8,128)(2,1)}, bf16[128,512]{1,0:T(8,128)(2,1)}) custom-call(s32[3]{0:T(128)S(1)} %copy-done.3, bf16[384,128]{1,0:T(8,128)(2,1)S(1)} %get-tuple-element.89.refs_0_, bf16[384,128]{1,0:T(8,128)(2,1)S(1)} %collective-permute-done.15.refs_1_, ...), custom_call_target="tpu_custom_call" | custom-call | tf_op jit(solution)/shard_map/unpack_keys/pallas_call | solution.py:351
  (26 shorter events, 0.2 us)
Async XLA Ops:
  0.6 9.8 %copy-start.1 = (bf16[1,128,2048]{2,1,0:T(8,128)(2,1)S(1)}, bf16[1,128,2048]{2,1,0:T(8,128)(2,1)}, u32[]{:S(2)}) copy-start(bf16[1,128,2048]{2,1,0:T(8,128)(2,1)} %param.9) | copy-start | bytes 1572868
  4.7 8.0 %collective-permute-start = (bf16[640,128]{1,0:T(8,128)(2,1)}, bf16[640,128]{1,0:T(8,128)(2,1)S(1)}, u32[]{:S(2)}, u32[]{:S(2)}) collective-permute-start(bf16[640,128]{1,0:T(8,128)(2,1)} %get-tuple-element.59), channel_id=1, source_target_pairs={{0,32},{16,48},{32,64},{48,80},{64,96},{80,112},{96,0},{112,16},{1... | collective-permute-start | bytes 491528 | tf_op jit(solution)/shard_map/ppermute | solution.py:244
  6.2 10.4 %collective-permute-start.1 = (bf16[640,128]{1,0:T(8,128)(2,1)}, bf16[640,128]{1,0:T(8,128)(2,1)S(1)}, u32[]{:S(2)}, u32[]{:S(2)}) collective-permute-start(bf16[640,128]{1,0:T(8,128)(2,1)} %get-tuple-element.60), channel_id=1, source_target_pairs={{0,64},{16,80},{32,96},{48,112},{64,0},{80,16},{96,32},{112,48},{1... | collective-permute-start | bytes 491528 | tf_op jit(solution)/shard_map/ppermute | solution.py:244
  9.0 7.6 %collective-permute-start.2 = (bf16[640,128]{1,0:T(8,128)(2,1)}, bf16[640,128]{1,0:T(8,128)(2,1)S(1)}, u32[]{:S(2)}, u32[]{:S(2)}) collective-permute-start(bf16[640,128]{1,0:T(8,128)(2,1)} %get-tuple-element.61), channel_id=1, source_target_pairs={{0,96},{16,112},{32,0},{48,16},{64,32},{80,48},{96,64},{112,80},{1... | collective-permute-start | bytes 491528 | tf_op jit(solution)/shard_map/ppermute | solution.py:244
  10.4 0.6 copy-start.3
  11.0 1.0 %copy-start.2 = (bf16[1,128,2048]{2,1,0:T(8,128)(2,1)S(1)}, bf16[1,128,2048]{2,1,0:T(8,128)(2,1)}, u32[]{:S(2)}) copy-start(bf16[1,128,2048]{2,1,0:T(8,128)(2,1)} %param.12) | copy-start | bytes 1572868
  12.0 4.6 %copy-start.4 = (bf16[640,128]{1,0:T(8,128)(2,1)S(1)}, bf16[640,128]{1,0:T(8,128)(2,1)}, u32[]{:S(2)}) copy-start(bf16[640,128]{1,0:T(8,128)(2,1)} %get-tuple-element.62) | copy-start | bytes 491524
  16.8 15.0 %collective-permute-start.3 = (bf16[1536,128]{1,0:T(8,128)(2,1)S(1)}, bf16[1536,128]{1,0:T(8,128)(2,1)S(1)}, u32[]{:S(2)}, u32[]{:S(2)}) collective-permute-start(bf16[1536,128]{1,0:T(8,128)(2,1)S(1)} %pad_maximum_fusion), channel_id=1, source_target_pairs={{0,128},{128,0},{1,129},{129,1},{2,130},{130,2},{3,131},{131,3},{4... | collective-permute-start | bytes 1179656 | tf_op jit(solution)/shard_map/ppermute | solution.py:254
  17.2 9.3 %collective-permute-start.4 = (bf16[256,512]{1,0:T(8,128)(2,1)S(1)}, bf16[256,512]{1,0:T(8,128)(2,1)S(1)}, u32[]{:S(2)}, u32[]{:S(2)}) collective-permute-start(bf16[256,512]{1,0:T(8,128)(2,1)S(1)} %get-tuple-element.71), channel_id=1, source_target_pairs={{0,32},{16,48},{32,64},{48,80},{64,96},{80,112},{96,0},{112,16},{1... | collective-permute-start | bytes 786440 | tf_op jit(solution)/shard_map/ppermute | solution.py:244
  18.6 13.2 %collective-permute-start.5 = (bf16[256,512]{1,0:T(8,128)(2,1)S(1)}, bf16[256,512]{1,0:T(8,128)(2,1)S(1)}, u32[]{:S(2)}, u32[]{:S(2)}) collective-permute-start(bf16[256,512]{1,0:T(8,128)(2,1)S(1)} %get-tuple-element.72), channel_id=1, source_target_pairs={{0,64},{16,80},{32,96},{48,112},{64,0},{80,16},{96,32},{112,48},{1... | collective-permute-start | bytes 786440 | tf_op jit(solution)/shard_map/ppermute | solution.py:244
  21.0 10.9 %collective-permute-start.6 = (bf16[256,512]{1,0:T(8,128)(2,1)S(1)}, bf16[256,512]{1,0:T(8,128)(2,1)S(1)}, u32[]{:S(2)}, u32[]{:S(2)}) collective-permute-start(bf16[256,512]{1,0:T(8,128)(2,1)S(1)} %get-tuple-element.73), channel_id=1, source_target_pairs={{0,96},{16,112},{32,0},{48,16},{64,32},{80,48},{96,64},{112,80},{1... | collective-permute-start | bytes 786440 | tf_op jit(solution)/shard_map/ppermute | solution.py:244
  22.5 11.0 %copy-start.5 = (bf16[2560,128]{1,0:T(8,128)(2,1)}, bf16[2560,128]{1,0:T(8,128)(2,1)S(1)}, u32[]{:S(2)}) copy-start(bf16[2560,128]{1,0:T(8,128)(2,1)S(1)} %slice_dynamic-update-slice_fusion.refs_4_) | copy-start | bytes 1966084
  22.5 9.3 %collective-permute-start.7 = (bf16[2560,128]{1,0:T(8,128)(2,1)S(1)}, bf16[2560,128]{1,0:T(8,128)(2,1)S(1)}, u32[]{:S(2)}, u32[]{:S(2)}) collective-permute-start(bf16[2560,128]{1,0:T(8,128)(2,1)S(1)} %slice_dynamic-update-slice_fusion.refs_4_), channel_id=1, source_target_pairs={{0,16},{16,0},{32,48},{48,32},{64,80},{80,64},{96,112},{112,96},{1... | collective-permute-start | bytes 1966088 | tf_op jit(solution)/shard_map/ppermute | solution.py:250
  31.8 1.7 %collective-permute-start.8 = (bf16[1536,128]{1,0:T(8,128)(2,1)S(1)}, bf16[1536,128]{1,0:T(8,128)(2,1)S(1)}, u32[]{:S(2)}, u32[]{:S(2)}) collective-permute-start(bf16[1536,128]{1,0:T(8,128)(2,1)S(1)} %collective-permute-done.3.refs_6_), channel_id=1, source_target_pairs={{0,16},{16,0},{32,48},{48,32},{64,80},{80,64},{96,112},{112,96},{1... | collective-permute-start | bytes 1179656 | tf_op jit(solution)/shard_map/ppermute | solution.py:250
  31.8 1.7 %copy-start.6 = (bf16[2560,128]{1,0:T(8,128)(2,1)}, bf16[2560,128]{1,0:T(8,128)(2,1)S(1)}, u32[]{:S(2)}) copy-start(bf16[2560,128]{1,0:T(8,128)(2,1)S(1)} %collective-permute-done.7.refs_5_) | copy-start | bytes 1966084
  64.4 1.7 %collective-permute-start.13 = (bf16[1536,128]{1,0:T(8,128)(2,1)S(1)}, bf16[1536,128]{1,0:T(8,128)(2,1)S(1)}, u32[]{:S(2)}, u32[]{:S(2)}) collective-permute-start(bf16[1536,128]{1,0:T(8,128)(2,1)S(1)} %get-tuple-element.88), channel_id=1, source_target_pairs={{0,16},{16,0},{32,48},{48,32},{64,80},{80,64},{96,112},{112,96},{1... | collective-permute-start | bytes 1179656 | tf_op jit(solution)/shard_map/ppermute | solution.py:250
  64.6 9.7 %collective-permute-start.12 = (bf16[2560,128]{1,0:T(8,128)(2,1)}, bf16[2560,128]{1,0:T(8,128)(2,1)S(1)}, u32[]{:S(2)}, u32[]{:S(2)}) collective-permute-start(bf16[2560,128]{1,0:T(8,128)(2,1)} %get-tuple-element.86), channel_id=1, source_target_pairs={{0,16},{16,0},{32,48},{48,32},{64,80},{80,64},{96,112},{112,96},{1... | collective-permute-start | bytes 1966088 | tf_op jit(solution)/shard_map/ppermute | solution.py:250
  67.4 12.8 %copy-start = (f32[1536,128]{1,0:T(8,128)S(1)}, f32[1536,128]{1,0:T(8,128)}, u32[]{:S(2)}) copy-start(f32[1536,128]{1,0:T(8,128)} %get-tuple-element.85.own) | copy-start | bytes 2359300
  67.4 12.7 %collective-permute-start.14 = (bf16[1536,128]{1,0:T(8,128)(2,1)S(1)}, bf16[1536,128]{1,0:T(8,128)(2,1)S(1)}, u32[]{:S(2)}, u32[]{:S(2)}) collective-permute-start(bf16[1536,128]{1,0:T(8,128)(2,1)S(1)} %add_convert_fusion), channel_id=1, source_target_pairs={{0,128},{128,0},{1,129},{129,1},{2,130},{130,2},{3,131},{131,3},{4... | collective-permute-start | bytes 1179656 | tf_op jit(solution)/shard_map/ppermute | solution.py:254
  70.6 14.6 %collective-permute-start.9 = (bf16[256,512]{1,0:T(8,128)(2,1)S(1)}, bf16[256,512]{1,0:T(8,128)(2,1)S(1)}, u32[]{:S(2)}, u32[]{:S(2)}) collective-permute-start(bf16[256,512]{1,0:T(8,128)(2,1)S(1)} %get-tuple-element.80), channel_id=1, source_target_pairs={{0,96},{16,112},{32,0},{48,16},{64,32},{80,48},{96,64},{112,80},{1... | collective-permute-start | bytes 786440 | tf_op jit(solution)/shard_map/ppermute | solution.py:244
  73.0 12.9 %collective-permute-start.10 = (bf16[256,512]{1,0:T(8,128)(2,1)S(1)}, bf16[256,512]{1,0:T(8,128)(2,1)S(1)}, u32[]{:S(2)}, u32[]{:S(2)}) collective-permute-start(bf16[256,512]{1,0:T(8,128)(2,1)S(1)} %get-tuple-element.81), channel_id=1, source_target_pairs={{0,64},{16,80},{32,96},{48,112},{64,0},{80,16},{96,32},{112,48},{1... | collective-permute-start | bytes 786440 | tf_op jit(solution)/shard_map/ppermute | solution.py:244
  74.2 15.7 %collective-permute-start.11 = (bf16[256,512]{1,0:T(8,128)(2,1)S(1)}, bf16[256,512]{1,0:T(8,128)(2,1)S(1)}, u32[]{:S(2)}, u32[]{:S(2)}) collective-permute-start(bf16[256,512]{1,0:T(8,128)(2,1)S(1)} %get-tuple-element.82), channel_id=1, source_target_pairs={{0,32},{16,48},{32,64},{48,80},{64,96},{80,112},{96,0},{112,16},{1... | collective-permute-start | bytes 786440 | tf_op jit(solution)/shard_map/ppermute | solution.py:244
  74.3 16.7 %collective-permute-start.18 = (bf16[256,128]{1,0:T(8,128)(2,1)S(1)}, bf16[256,128]{1,0:T(8,128)(2,1)S(1)}, u32[]{:S(2)}, u32[]{:S(2)}) collective-permute-start(bf16[256,128]{1,0:T(8,128)(2,1)S(1)} %get-tuple-element.95), channel_id=1, source_target_pairs={{0,96},{16,112},{32,0},{48,16},{64,32},{80,48},{96,64},{112,80},{1... | collective-permute-start | bytes 196616 | tf_op jit(solution)/shard_map/ppermute | solution.py:244
  80.2 16.2 %collective-permute-start.15 = (bf16[384,128]{1,0:T(8,128)(2,1)S(1)}, bf16[384,128]{1,0:T(8,128)(2,1)S(1)}, u32[]{:S(2)}, u32[]{:S(2)}) collective-permute-start(bf16[384,128]{1,0:T(8,128)(2,1)S(1)} %get-tuple-element.90), channel_id=1, source_target_pairs={{0,96},{16,112},{32,0},{48,16},{64,32},{80,48},{96,64},{112,80},{1... | collective-permute-start | bytes 294920 | tf_op jit(solution)/shard_map/ppermute | solution.py:244
  85.2 11.2 %collective-permute-start.16 = (bf16[384,128]{1,0:T(8,128)(2,1)S(1)}, bf16[384,128]{1,0:T(8,128)(2,1)S(1)}, u32[]{:S(2)}, u32[]{:S(2)}) collective-permute-start(bf16[384,128]{1,0:T(8,128)(2,1)S(1)} %get-tuple-element.91), channel_id=1, source_target_pairs={{0,64},{16,80},{32,96},{48,112},{64,0},{80,16},{96,32},{112,48},{1... | collective-permute-start | bytes 294920 | tf_op jit(solution)/shard_map/ppermute | solution.py:244
  85.9 10.5 %collective-permute-start.17 = (bf16[384,128]{1,0:T(8,128)(2,1)S(1)}, bf16[384,128]{1,0:T(8,128)(2,1)S(1)}, u32[]{:S(2)}, u32[]{:S(2)}) collective-permute-start(bf16[384,128]{1,0:T(8,128)(2,1)S(1)} %get-tuple-element.92), channel_id=1, source_target_pairs={{0,32},{16,48},{32,64},{48,80},{64,96},{80,112},{96,0},{112,16},{1... | collective-permute-start | bytes 294920 | tf_op jit(solution)/shard_map/ppermute | solution.py:244
  89.9 5.8 %collective-permute-start.19 = (bf16[256,128]{1,0:T(8,128)(2,1)S(1)}, bf16[256,128]{1,0:T(8,128)(2,1)S(1)}, u32[]{:S(2)}, u32[]{:S(2)}) collective-permute-start(bf16[256,128]{1,0:T(8,128)(2,1)S(1)} %get-tuple-element.96), channel_id=1, source_target_pairs={{0,64},{16,80},{32,96},{48,112},{64,0},{80,16},{96,32},{112,48},{1... | collective-permute-start | bytes 196616 | tf_op jit(solution)/shard_map/ppermute | solution.py:244
  91.0 5.5 %collective-permute-start.20 = (bf16[256,128]{1,0:T(8,128)(2,1)S(1)}, bf16[256,128]{1,0:T(8,128)(2,1)S(1)}, u32[]{:S(2)}, u32[]{:S(2)}) collective-permute-start(bf16[256,128]{1,0:T(8,128)(2,1)S(1)} %get-tuple-element.97), channel_id=1, source_target_pairs={{0,32},{16,48},{32,64},{48,80},{64,96},{80,112},{96,0},{112,16},{1... | collective-permute-start | bytes 196616 | tf_op jit(solution)/shard_map/ppermute | solution.py:244
